TPU v7x, 32 devices: a whole 2x2x4 slice. The times are simulated.
32 devices in a mesh: gx: 8 (over z, x), row: 2 (over core), th: 2 (over y).
Axes of the slice: x: 2, y: 2, z: 4, core: 2. Of those that a mesh axis runs over, the one named last changes fastest.
Arguments:
- state: float32 [5, 256, 32, 256], P(None, 'gx', 'row', 'th'), may hold values from -2 to 4, as said below
- adjoint_seed: float32 [5, 256, 32, 256], P(None, 'gx', 'row', 'th'), may hold values from -6 to 6
- coef_x: float32 [9], replicated, may hold values from -1.75 to 1.75
- coef_r: float32 [9], replicated, may hold values from -1.75 to 1.75
- coef_t: float32 [9], replicated, may hold values from -1.75 to 1.75
- coef_filter: float32 [9], replicated, may hold values from -0.625 to 0.625
- metric: float32 [32], P('row'), may hold values from 0.5 to 2
Outputs:
- new_state: float32 [5, 256, 32, 256], P(None, 'gx', 'row', 'th')
- adjoint_state: float32 [5, 256, 32, 256], P(None, 'gx', 'row', 'th')
Inputs may be any that keep to these rules, and one draw needn't show every extreme that they name: `state`: component 0 (density) lies in [0.5, 1.5], components 1 to 3 (momenta) in [-2, 2], component 4 (total energy) in [2, 4].
All inputs are finite; a program needn't handle non-finite values.
Results may differ from a plain program's by a relative error of at most 0.0001.
Values sent between devices are 32-bit elements; how exact they have to be, the bound alone decides.
A program may use at most 64 MiB of HBM per device.

v0:
```python
import jax
import jax.numpy as jnp
from jax import lax
from jax.sharding import PartitionSpec as P

section_dt = 0.1
gamma_less = 0.4
highest = lax.Precision.HIGHEST


def extended(cells, sides, width):
    for axis, dim in sides:
        count = lax.axis_size(axis)
        ends = count - 1
        head = lax.slice_in_dim(cells, 0, width, axis=dim)
        tail = lax.slice_in_dim(cells, cells.shape[dim] - width, cells.shape[dim], axis=dim)
        cells = jnp.concatenate(
            [
                lax.ppermute(tail, axis, [(i, (i + 1) % count) for i in range(ends)]),
                cells,
                lax.ppermute(head, axis, [((i + 1) % count, i) for i in range(ends)]),
            ],
            axis=dim,
        )
    return cells


def from_partner(value, axis, bit):
    mask = 2**bit
    pairs = [(source, source ^ mask) for source in range(lax.axis_size(axis))]
    return lax.ppermute(value, axis, pairs)


def fluxes(state):
    density = state[0]
    velocity = state[1:4] / density
    pressure = gamma_less * (state[4] - 0.5 * jnp.sum(state[1:4] * velocity, axis=0))
    enthalpy = state[4] + pressure
    result = []
    for direction in range(3):
        speed = velocity[direction]
        moment = state[1:4] * speed
        moment = moment.at[direction].add(pressure)
        result.append(
            jnp.concatenate([state[1 + direction][None], moment, (enthalpy * speed)[None]], axis=0)
        )
    return result


def band_matrix(coef, count):
    taps = coef.shape[0]
    rows = lax.broadcasted_iota(jnp.int32, (count + taps - 1, count), 0)
    cols = lax.broadcasted_iota(jnp.int32, (count + taps - 1, count), 1)
    offset = rows - cols
    picks = jnp.arange(taps, dtype=jnp.int32)
    hits = offset[None, :, :] == picks[:, None, None]
    return jnp.sum(jnp.where(hits, coef[:, None, None], 0.0), axis=0)


def along_x(ext, band):
    return jnp.einsum("vard,ai->vird", ext, band, precision=highest)


def along_r(ext, band):
    return jnp.einsum("vxad,ai->vxid", ext, band, precision=highest)


def along_t(ext, band):
    return jnp.einsum("vxra,ai->vxri", ext, band, precision=highest)


def shards(state, adjoint_seed, coef_x, coef_r, coef_t, coef_filter, metric):
    cells_x = state.shape[1]
    cells_r = state.shape[2]
    cells_t = state.shape[3]
    reach = (coef_x.shape[0] - 1) // 2
    weight_r = metric[None, None, :, None]
    flux_x, flux_r, flux_t = fluxes(state)
    wide_x = extended(flux_x, (("gx", 1),), reach)
    wide_r = extended(flux_r, (("row", 2),), reach)
    rims = jnp.concatenate([flux_t[..., cells_t - reach :], flux_t[..., :reach]], axis=3)
    other = from_partner(rims, "th", 0)
    wide_t = jnp.concatenate([other[..., :reach], flux_t, other[..., reach:]], axis=3)
    resid = -(
        along_x(wide_x, band_matrix(coef_x, cells_x))
        + along_r(wide_r, band_matrix(coef_r, cells_r))
        + weight_r * along_t(wide_t, band_matrix(coef_t, cells_t))
    )
    section = state + section_dt * resid
    wide_section = extended(section, (("gx", 1),), reach)
    new_state = section - along_x(wide_section, band_matrix(coef_filter, cells_x))
    flip_filter = coef_filter[::-1]
    flip_x = coef_x[::-1]
    wide_seed = extended(adjoint_seed, (("gx", 1),), reach)
    lam_section = adjoint_seed - along_x(wide_seed, band_matrix(flip_filter, cells_x))
    lam_resid = section_dt * lam_section
    wide_lam = extended(lam_resid, (("gx", 1),), reach)
    grad_x = -along_x(wide_lam, band_matrix(flip_x, cells_x))
    wide_lam_r = extended(lam_resid, (("row", 2),), reach)
    grad_r = -along_r(wide_lam_r, band_matrix(coef_r[::-1], cells_r))
    weighted = weight_r * lam_resid
    rims_back = jnp.concatenate([weighted[..., cells_t - reach :], weighted[..., :reach]], axis=3)
    other_back = from_partner(rims_back, "th", 0)
    wide_lam_t = jnp.concatenate(
        [other_back[..., :reach], weighted, other_back[..., reach:]], axis=3
    )
    grad_t = -along_t(wide_lam_t, band_matrix(coef_t[::-1], cells_t))
    _, pull = jax.vjp(fluxes, state)
    (flux_grad,) = pull([grad_x, grad_r, grad_t])
    adjoint_state = lam_section + flux_grad
    return (new_state, adjoint_state)


def solution(mesh):
    placed = (P(None, "gx", "row", "th"), P(None, "gx", "row", "th"), P(), P(), P(), P(), P("row"))
    return jax.shard_map(
        shards,
        mesh=mesh,
        in_specs=placed,
        out_specs=(P(None, "gx", "row", "th"), P(None, "gx", "row", "th")),
        check_vma=False,
    )
```

profile of v0, /device:TPU:9, one launch (start us, length us, event | category | flops | bytes accessed | tf_op | source)
XLA Modules:
  0.0 119.1 jit_solution(17861379795461267805)
XLA Ops:
  0.7 1.8 %copy.79 = f32[5,32,16,128]{3,1,2,0:T(8,128)S(1)} copy(f32[5,32,16,128]{3,2,1,0:T(8,128)} %param.14) | data formatting | bytes 2621440 | tf_op args[1]
  3.6 3.1 %collective-permute-start.7 = (f32[5,4,16,128]{3,1,2,0:T(4,128)S(1)}, f32[5,4,16,128]{3,1,2,0:T(4,128)S(1)}, u32[]{:S(2)}, u32[]{:S(2)}) collective-permute-start(f32[5,4,16,128]{3,1,2,0:T(4,128)S(1)} %get-tuple-element.95), channel_id=1, source_target_pairs={{0,4},{4,8},{8,12},{12,16},{16,20},{20,24},{24,28},{1,5},{5,9},{9,... | collective-permute-start | bytes 491528 | tf_op jit(solution)/shard_map/ppermute | solution.py:19
  6.8 3.1 %collective-permute-start.8 = (f32[5,4,16,128]{3,1,2,0:T(4,128)S(1)}, f32[5,4,16,128]{3,1,2,0:T(4,128)S(1)}, u32[]{:S(2)}, u32[]{:S(2)}) collective-permute-start(f32[5,4,16,128]{3,1,2,0:T(4,128)S(1)} %get-tuple-element.96), channel_id=1, source_target_pairs={{4,0},{8,4},{12,8},{16,12},{20,16},{24,20},{28,24},{5,1},{9,5},{13... | collective-permute-start | bytes 491528 | tf_op jit(solution)/shard_map/ppermute | solution.py:21
  16.0 4.3 %broadcast_multiply_fusion.1 = (f32[5,32,16,128]{3,1,2,0:T(8,128)S(1)}, f32[5,32,16,128]{3,1,2,0:T(8,128)S(1)}, f32[5,32,16,128]{3,1,2,0:T(8,128)}) fusion(f32[16]{0:T(128)S(1)} %broadcast_multiply_fusion.6, f32[5,32,16,128]{3,1,2,0:T(8,128)} %copy-done, f32[5,4,16,128]{3,1,2,0:T(4,128)S(1)} %collective-permute-done.8, ...), kind=kOutput, calls=%fused_computation.78 | convolution fusion | flops 159088640 | bytes 5575744 | tf_op jit(solution)/shard_map/vard,ai->vird/dot_general | solution.py:61
  21.1 2.0 %fusion.122 = (f32[5,32,16,4]{3,1,2,0:T(8,128)}, f32[5,32,16,4]{3,1,2,0:T(8,128)}) fusion(f32[5,32,16,128]{3,1,2,0:T(8,128)S(1)} %get-tuple-element.92), kind=kLoop, calls=%fused_computation.161 | loop fusion | bytes 163840 | tf_op jit(solution)/shard_map/slice | solution.py:102
  23.0 1.9 %copy.80 = f32[5,32,16,4]{1,3,2,0:T(4,128)S(1)} copy(f32[5,32,16,4]{3,1,2,0:T(8,128)} %get-tuple-element.93) | data formatting | bytes 81920 | tf_op jit(solution)/shard_map/slice | solution.py:102
  24.9 1.9 %copy.81 = f32[5,32,16,4]{1,3,2,0:T(4,128)S(1)} copy(f32[5,32,16,4]{3,1,2,0:T(8,128)} %get-tuple-element.94) | data formatting | bytes 81920 | tf_op jit(solution)/shard_map/slice | solution.py:102
  29.0 1.9 %collective-permute-start.12 = (f32[5,4,16,128]{3,1,2,0:T(4,128)}, f32[5,4,16,128]{3,1,2,0:T(4,128)}, u32[]{:S(2)}, u32[]{:S(2)}) collective-permute-start(f32[5,4,16,128]{3,1,2,0:T(4,128)} %get-tuple-element.87), channel_id=1, source_target_pairs={{0,4},{4,8},{8,12},{12,16},{16,20},{20,24},{24,28},{1,5},{5,9},{9,... | collective-permute-start | bytes 491528 | tf_op jit(solution)/shard_map/ppermute | solution.py:19
  30.9 4.3 %collective-permute-start.13 = (f32[5,4,16,128]{3,1,2,0:T(4,128)}, f32[5,4,16,128]{3,1,2,0:T(4,128)}, u32[]{:S(2)}, u32[]{:S(2)}) collective-permute-start(f32[5,4,16,128]{3,1,2,0:T(4,128)} %get-tuple-element.88), channel_id=1, source_target_pairs={{4,0},{8,4},{12,8},{16,12},{20,16},{24,20},{28,24},{5,1},{9,5},{13... | collective-permute-start | bytes 491528 | tf_op jit(solution)/shard_map/ppermute | solution.py:21
  36.5 4.8 %collective-permute-start.11 = (f32[5,32,4,128]{3,1,2,0:T(8,128)S(1)}, f32[5,32,4,128]{3,1,2,0:T(8,128)}, u32[]{:S(2)}, u32[]{:S(2)}) collective-permute-start(f32[5,32,4,128]{3,1,2,0:T(8,128)S(1)} %get-tuple-element.90), channel_id=1, source_target_pairs={{2,0},{3,1},{6,4},{7,5},{10,8},{11,9},{14,12},{15,13},{18,16},{19,... | collective-permute-start | bytes 983048 | tf_op jit(solution)/shard_map/ppermute | solution.py:21
  41.3 1.6 %copy.105 = f32[5,32,16,4]{3,1,2,0:T(8,128)} copy(f32[5,32,16,4]{1,3,2,0:T(4,128)S(1)} %get-tuple-element.105) | data formatting | bytes 81920
  42.9 1.6 %copy.106 = f32[5,32,16,4]{3,1,2,0:T(8,128)} copy(f32[5,32,16,4]{1,3,2,0:T(4,128)S(1)} %get-tuple-element.106) | data formatting | bytes 81920
  44.5 4.3 %fusion.63 = f32[5,32,16,128]{3,1,2,0:T(8,128)S(1)} fusion(f32[5,32,16,4]{3,1,2,0:T(8,128)} %copy.106, f32[5,32,16,128]{3,1,2,0:T(8,128)S(1)} %get-tuple-element.92, f32[5,32,16,4]{3,1,2,0:T(8,128)} %copy.105, f32[136,128]{1,0:T(8,128)S(1)} %copy-done.25), kind=kOutput, calls=%fused_computation.55 | convolution fusion | flops 535797760 | bytes 2772992 | tf_op jit(solution)/shard_map/vxra,ai->vxri/dot_general | solution.py:69
  48.9 2.3 %fusion.51 = f32[5,32,16,128]{3,1,2,0:T(8,128)S(1)} fusion(f32[5,4,16,128]{3,1,2,0:T(4,128)} %collective-permute-done.13, f32[5,32,16,128]{3,1,2,0:T(8,128)S(1)} %get-tuple-element.91, f32[5,4,16,128]{3,1,2,0:T(4,128)} %collective-permute-done.12, f32[40,32]{0,1:T(8,128)S(1)} %copy-done.28), kind=kOutput, calls=%fused_computation.51 | convolution fusion | flops 158433280 | bytes 2954240 | tf_op jit(solution)/shard_map/vard,ai->vird/dot_general | solution.py:61
  52.5 2.3 %fusion.16 = f32[16,5,32,128]{3,0,2,1:T(8,128)S(1)} fusion(f32[5,32,24,128]{3,1,2,0:T(8,128)S(1)} %pad_maximum_fusion.1, f32[24,16]{0,1:T(8,128)S(1)} %copy-done.30), kind=kOutput, calls=%fused_computation.18 | convolution fusion | flops 94371840 | bytes 3278336 | tf_op jit(solution)/shard_map/vxad,ai->vxid/dot_general | solution.py:65
  60.9 1.8 %fusion.91 = (f32[3,32,16,128]{3,1,2,0:T(8,128)}, f32[32,16,128]{2,0,1:T(8,128)S(1)}, f32[3,32,16,128]{3,1,2,0:T(8,128)S(1)}, f32[3,32,16,128]{3,1,2,0:T(8,128)S...) fusion(f32[1,32,16,128]{3,1,2,0:T(8,128)S(1)} %get-tuple-element.72, ...), kind=kLoop, calls=%fused_computation.82 | loop fusion | flops 2490368 | bytes 9699328 | tf_op jit(solution)/shard_map/transpose(jvp())/div | solution.py:36
  64.5 1.9 %collective-permute-start = (f32[5,4,16,128]{3,1,2,0:T(4,128)}, f32[5,4,16,128]{3,1,2,0:T(4,128)}, u32[]{:S(2)}, u32[]{:S(2)}) collective-permute-start(f32[5,4,16,128]{3,1,2,0:T(4,128)} %get-tuple-element.83), channel_id=1, source_target_pairs={{0,4},{4,8},{8,12},{12,16},{16,20},{20,24},{24,28},{1,5},{5,9},{9,... | collective-permute-start | bytes 491528 | tf_op jit(solution)/shard_map/ppermute | solution.py:19
  66.4 4.5 %collective-permute-start.1 = (f32[5,4,16,128]{3,1,2,0:T(4,128)}, f32[5,4,16,128]{3,1,2,0:T(4,128)}, u32[]{:S(2)}, u32[]{:S(2)}) collective-permute-start(f32[5,4,16,128]{3,1,2,0:T(4,128)} %get-tuple-element.84), channel_id=1, source_target_pairs={{4,0},{8,4},{12,8},{16,12},{20,16},{24,20},{28,24},{5,1},{9,5},{13... | collective-permute-start | bytes 491528 | tf_op jit(solution)/shard_map/ppermute | solution.py:21
  72.6 2.5 %copy.69 = f32[5,32,16,4]{1,3,2,0:T(4,128)} copy(f32[5,32,16,4]{3,1,2,0:T(8,128)} %get-tuple-element.85) | data formatting | bytes 81920 | tf_op jit(solution)/shard_map/slice | solution.py:81
  77.7 1.8 %pad_maximum_fusion.5 = (f32[5,32,4,128]{3,1,2,0:T(8,128)}, f32[5,32,4,128]{3,1,2,0:T(8,128)}) fusion(f32[1,32,16,128]{3,1,2,0:T(8,128)S(1)} %get-tuple-element.98, f32[3,32,16,128]{3,1,2,0:T(8,128)S(1)} %get-tuple-element.109, f32[1,32,16,128]{3,1,2,0:T(8,128)} %get-tuple-element.65), kind=kLoop, calls=%fused_computation.90 | loop fusion | flops 327680 | bytes 1966080 | tf_op jit(solution)/shard_map/slice | solution.py:16
  80.7 4.5 %collective-permute-start.3 = (f32[5,32,4,128]{3,1,2,0:T(8,128)}, f32[5,32,4,128]{3,1,2,0:T(8,128)}, u32[]{:S(2)}, u32[]{:S(2)}) collective-permute-start(f32[5,32,4,128]{3,1,2,0:T(8,128)} %get-tuple-element.82), channel_id=1, source_target_pairs={{2,0},{3,1},{6,4},{7,5},{10,8},{11,9},{14,12},{15,13},{18,16},{19,... | collective-permute-start | bytes 983048 | tf_op jit(solution)/shard_map/ppermute | solution.py:21
  85.2 1.7 %collective-permute-done.4 = f32[5,32,16,8]{1,3,2,0:T(8,128)S(1)} collective-permute-done((f32[5,32,16,8]{1,3,2,0:T(8,128)S(1)}, f32[5,32,16,8]{1,3,2,0:T(8,128)S(1)}, u32[]{:S(2)}, u32[]{:S(2)}) %collective-permute-start.4) | collective-permute-done | bytes 81952 | tf_op jit(solution)/shard_map/ppermute | solution.py:31
  87.6 2.6 %copy.103 = f32[5,32,16,4]{3,1,2,0:T(8,128)} copy(f32[5,32,16,4]{1,3,2,0:T(4,128)} %get-tuple-element.103) | data formatting | bytes 81920
  90.3 1.6 %copy.104 = f32[5,32,16,4]{3,1,2,0:T(8,128)} copy(f32[5,32,16,4]{1,3,2,0:T(4,128)S(1)} %get-tuple-element.104) | data formatting | bytes 81920
  91.9 4.4 %fusion.87 = f32[5,32,16,128]{3,1,2,0:T(8,128)S(1)} fusion(f32[5,32,16,4]{3,1,2,0:T(8,128)} %copy.104, f32[1,32,16,128]{3,1,2,0:T(8,128)S(1)} %copy-done.20, f32[3,32,16,128]{3,1,2,0:T(8,128)S(1)} %copy-done.6, f32[1,32,16,128]{3,1,2,0:T(8,128)} %copy-done.24, f32[5,32,16,4]{3,1,2,0:T(8,128)} %copy.103, f32[16]{0:T(128)S(1)} %copy-done.36, ...), kind=kOutput, calls=%fused_computation.63 | convolution fusion | flops 536494080 | bytes 2773056 | tf_op jit(solution)/shard_map/vxra,ai->vxri/dot_general | solution.py:69
  97.7 2.3 %fusion.18 = f32[16,5,32,128]{3,0,2,1:T(8,128)S(1)} fusion(f32[5,32,24,128]{3,1,2,0:T(8,128)S(1)} %pad_maximum_fusion, f32[24,16]{0,1:T(8,128)S(1)} %copy-done.29), kind=kOutput, calls=%fused_computation.20 | convolution fusion | flops 94371840 | bytes 3278336 | tf_op jit(solution)/shard_map/vxad,ai->vxid/dot_general | solution.py:65
  100.2 3.3 %fusion.84 = f32[5,32,16,128]{3,1,2,0:T(8,128)S(1)} fusion(f32[5,32,16,128]{3,1,2,0:T(8,128)S(1)} %fusion.87, f32[5,4,16,128]{3,1,2,0:T(4,128)} %collective-permute-done.1, f32[1,32,16,128]{3,1,2,0:T(8,128)S(1)} %get-tuple-element.99, f32[3,32,16,128]{3,1,2,0:T(8,128)S(1)} %get-tuple-element.111, f32[1,32,16,128]{3,1,2,0:T(8,128)S(1)} %copy-done.13, ...), kind=kOutput, calls=%fused_computation.62 | convolution fusion | flops 160563200 | bytes 6886400 | tf_op jit(solution)/shard_map/vard,ai->vird/dot_general | solution.py:61
  103.6 1.9 %collective-permute-start.5 = (f32[5,4,16,128]{3,1,2,0:T(4,128)S(1)}, f32[5,4,16,128]{3,1,2,0:T(4,128)S(1)}, u32[]{:S(2)}, u32[]{:S(2)}) collective-permute-start(f32[5,4,16,128]{3,1,2,0:T(4,128)S(1)} %get-tuple-element.79), channel_id=1, source_target_pairs={{0,4},{4,8},{8,12},{12,16},{16,20},{20,24},{24,28},{1,5},{5,9},{9,... | collective-permute-start | bytes 491528 | tf_op jit(solution)/shard_map/ppermute | solution.py:19
  105.5 4.5 %collective-permute-start.6 = (f32[5,4,16,128]{3,1,2,0:T(4,128)S(1)}, f32[5,4,16,128]{3,1,2,0:T(4,128)S(1)}, u32[]{:S(2)}, u32[]{:S(2)}) collective-permute-start(f32[5,4,16,128]{3,1,2,0:T(4,128)S(1)} %get-tuple-element.80), channel_id=1, source_target_pairs={{4,0},{8,4},{12,8},{16,12},{20,16},{24,20},{28,24},{5,1},{9,5},{13... | collective-permute-start | bytes 491528 | tf_op jit(solution)/shard_map/ppermute | solution.py:21
  111.0 1.8 %copy.90 = f32[5,32,16,128]{3,2,1,0:T(8,128)} copy(f32[5,32,16,128]{3,1,2,0:T(8,128)S(1)} %add_add_fusion) | data formatting | bytes 2621440
  112.8 3.2 %collective-permute-done.6 = f32[5,4,16,128]{3,1,2,0:T(4,128)S(1)} collective-permute-done((f32[5,4,16,128]{3,1,2,0:T(4,128)S(1)}, f32[5,4,16,128]{3,1,2,0:T(4,128)S(1)}, u32[]{:S(2)}, u32[]{:S(2)}) %collective-permute-start.6) | collective-permute-done | bytes 163872 | tf_op jit(solution)/shard_map/ppermute | solution.py:21
  117.3 1.8 %copy.89 = f32[5,32,16,128]{3,2,1,0:T(8,128)} copy(f32[5,32,16,128]{3,1,2,0:T(8,128)S(1)} %fusion.69) | data formatting | bytes 2621440
  (130 shorter events, 30.4 us)
Async XLA Ops:
  0.6 9.3 %copy-start.34 = (f32[9]{0:T(128)S(1)}, f32[9]{0:T(128)}, u32[]{:S(2)}) copy-start(f32[9]{0:T(128)} %param.16) | copy-start | bytes 112
  0.7 9.4 %copy-start.32 = (f32[9]{0:T(128)S(1)}, f32[9]{0:T(128)}, u32[]{:S(2)}) copy-start(f32[9]{0:T(128)} %param.18) | copy-start | bytes 112
  0.7 9.5 %copy-start.35 = (f32[16]{0:T(128)S(1)}, f32[16]{0:T(128)}, u32[]{:S(2)}) copy-start(f32[16]{0:T(128)} %param.19) | copy-start | bytes 196
  0.7 9.5 %copy-start.2 = (f32[5,32,16,128]{3,2,1,0:T(8,128)S(1)}, f32[5,32,16,128]{3,2,1,0:T(8,128)}, u32[]{:S(2)}) copy-start(f32[5,32,16,128]{3,2,1,0:T(8,128)} %param.13) | copy-start | bytes 3932164
  3.6 11.3 %collective-permute-start.7 = (f32[5,4,16,128]{3,1,2,0:T(4,128)S(1)}, f32[5,4,16,128]{3,1,2,0:T(4,128)S(1)}, u32[]{:S(2)}, u32[]{:S(2)}) collective-permute-start(f32[5,4,16,128]{3,1,2,0:T(4,128)S(1)} %get-tuple-element.95), channel_id=1, source_target_pairs={{0,4},{4,8},{8,12},{12,16},{16,20},{20,24},{24,28},{1,5},{5,9},{9,... | collective-permute-start | bytes 491528 | tf_op jit(solution)/shard_map/ppermute | solution.py:19
  6.8 9.3 %collective-permute-start.8 = (f32[5,4,16,128]{3,1,2,0:T(4,128)S(1)}, f32[5,4,16,128]{3,1,2,0:T(4,128)S(1)}, u32[]{:S(2)}, u32[]{:S(2)}) collective-permute-start(f32[5,4,16,128]{3,1,2,0:T(4,128)S(1)} %get-tuple-element.96), channel_id=1, source_target_pairs={{4,0},{8,4},{12,8},{16,12},{20,16},{24,20},{28,24},{5,1},{9,5},{13... | collective-permute-start | bytes 491528 | tf_op jit(solution)/shard_map/ppermute | solution.py:21
  26.9 14.4 %collective-permute-start.9 = (f32[5,32,16,8]{1,3,2,0:T(8,128)S(1)}, f32[5,32,16,8]{1,3,2,0:T(8,128)S(1)}, u32[]{:S(2)}, u32[]{:S(2)}) collective-permute-start(f32[5,32,16,8]{1,3,2,0:T(8,128)S(1)} %pad_maximum_fusion.7), channel_id=1, source_target_pairs={{0,1},{1,0},{2,3},{3,2},{4,5},{5,4},{6,7},{7,6},{8,9},{9,8},{10,11... | collective-permute-start | bytes 245768 | tf_op jit(solution)/shard_map/ppermute | solution.py:31
  29.0 19.9 %collective-permute-start.12 = (f32[5,4,16,128]{3,1,2,0:T(4,128)}, f32[5,4,16,128]{3,1,2,0:T(4,128)}, u32[]{:S(2)}, u32[]{:S(2)}) collective-permute-start(f32[5,4,16,128]{3,1,2,0:T(4,128)} %get-tuple-element.87), channel_id=1, source_target_pairs={{0,4},{4,8},{8,12},{12,16},{16,20},{20,24},{24,28},{1,5},{5,9},{9,... | collective-permute-start | bytes 491528 | tf_op jit(solution)/shard_map/ppermute | solution.py:19
  30.9 18.0 %collective-permute-start.13 = (f32[5,4,16,128]{3,1,2,0:T(4,128)}, f32[5,4,16,128]{3,1,2,0:T(4,128)}, u32[]{:S(2)}, u32[]{:S(2)}) collective-permute-start(f32[5,4,16,128]{3,1,2,0:T(4,128)} %get-tuple-element.88), channel_id=1, source_target_pairs={{4,0},{8,4},{12,8},{16,12},{20,16},{24,20},{28,24},{5,1},{9,5},{13... | collective-permute-start | bytes 491528 | tf_op jit(solution)/shard_map/ppermute | solution.py:21
  35.2 16.0 %collective-permute-start.10 = (f32[5,32,4,128]{3,1,2,0:T(8,128)}, f32[5,32,4,128]{3,1,2,0:T(8,128)}, u32[]{:S(2)}, u32[]{:S(2)}) collective-permute-start(f32[5,32,4,128]{3,1,2,0:T(8,128)} %get-tuple-element.89), channel_id=1, source_target_pairs={{0,2},{1,3},{4,6},{5,7},{8,10},{9,11},{12,14},{13,15},{16,18},{17,... | collective-permute-start | bytes 983048 | tf_op jit(solution)/shard_map/ppermute | solution.py:19
  36.5 14.8 %collective-permute-start.11 = (f32[5,32,4,128]{3,1,2,0:T(8,128)S(1)}, f32[5,32,4,128]{3,1,2,0:T(8,128)}, u32[]{:S(2)}, u32[]{:S(2)}) collective-permute-start(f32[5,32,4,128]{3,1,2,0:T(8,128)S(1)} %get-tuple-element.90), channel_id=1, source_target_pairs={{2,0},{3,1},{6,4},{7,5},{10,8},{11,9},{14,12},{15,13},{18,16},{19,... | collective-permute-start | bytes 983048 | tf_op jit(solution)/shard_map/ppermute | solution.py:21
  58.0 12.9 %copy-start.24 = (f32[1,32,16,128]{3,1,2,0:T(8,128)}, f32[1,32,16,128]{3,1,2,0:T(8,128)S(1)}, u32[]{:S(2)}) copy-start(f32[1,32,16,128]{3,1,2,0:T(8,128)S(1)} %get-tuple-element.67) | copy-start | bytes 786436
  60.9 10.0 %copy-start.19 = (f32[1,32,16,128]{3,1,2,0:T(8,128)}, f32[1,32,16,128]{3,1,2,0:T(8,128)S(1)}, u32[]{:S(2)}) copy-start(f32[1,32,16,128]{3,1,2,0:T(8,128)S(1)} %get-tuple-element.97) | copy-start | bytes 786436
  64.5 35.5 %collective-permute-start = (f32[5,4,16,128]{3,1,2,0:T(4,128)}, f32[5,4,16,128]{3,1,2,0:T(4,128)}, u32[]{:S(2)}, u32[]{:S(2)}) collective-permute-start(f32[5,4,16,128]{3,1,2,0:T(4,128)} %get-tuple-element.83), channel_id=1, source_target_pairs={{0,4},{4,8},{8,12},{12,16},{16,20},{20,24},{24,28},{1,5},{5,9},{9,... | collective-permute-start | bytes 491528 | tf_op jit(solution)/shard_map/ppermute | solution.py:19
  66.4 33.6 %collective-permute-start.1 = (f32[5,4,16,128]{3,1,2,0:T(4,128)}, f32[5,4,16,128]{3,1,2,0:T(4,128)}, u32[]{:S(2)}, u32[]{:S(2)}) collective-permute-start(f32[5,4,16,128]{3,1,2,0:T(4,128)} %get-tuple-element.84), channel_id=1, source_target_pairs={{4,0},{8,4},{12,8},{16,12},{20,16},{24,20},{28,24},{5,1},{9,5},{13... | collective-permute-start | bytes 491528 | tf_op jit(solution)/shard_map/ppermute | solution.py:21
  77.4 9.5 %collective-permute-start.4 = (f32[5,32,16,8]{1,3,2,0:T(8,128)S(1)}, f32[5,32,16,8]{1,3,2,0:T(8,128)S(1)}, u32[]{:S(2)}, u32[]{:S(2)}) collective-permute-start(f32[5,32,16,8]{1,3,2,0:T(8,128)S(1)} %pad_maximum_fusion.6), channel_id=1, source_target_pairs={{0,1},{1,0},{2,3},{3,2},{4,5},{5,4},{6,7},{7,6},{8,9},{9,8},{10,11... | collective-permute-start | bytes 245768 | tf_op jit(solution)/shard_map/ppermute | solution.py:31
  79.4 16.9 %collective-permute-start.2 = (f32[5,32,4,128]{3,1,2,0:T(8,128)}, f32[5,32,4,128]{3,1,2,0:T(8,128)}, u32[]{:S(2)}, u32[]{:S(2)}) collective-permute-start(f32[5,32,4,128]{3,1,2,0:T(8,128)} %get-tuple-element.81), channel_id=1, source_target_pairs={{0,2},{1,3},{4,6},{5,7},{8,10},{9,11},{12,14},{13,15},{16,18},{17,... | collective-permute-start | bytes 983048 | tf_op jit(solution)/shard_map/ppermute | solution.py:19
  80.7 15.6 %collective-permute-start.3 = (f32[5,32,4,128]{3,1,2,0:T(8,128)}, f32[5,32,4,128]{3,1,2,0:T(8,128)}, u32[]{:S(2)}, u32[]{:S(2)}) collective-permute-start(f32[5,32,4,128]{3,1,2,0:T(8,128)} %get-tuple-element.82), channel_id=1, source_target_pairs={{2,0},{3,1},{6,4},{7,5},{10,8},{11,9},{14,12},{15,13},{18,16},{19,... | collective-permute-start | bytes 983048 | tf_op jit(solution)/shard_map/ppermute | solution.py:21
  100.1 9.9 %copy-start.4 = (f32[5,32,16,128]{3,1,2,0:T(8,128)S(1)}, f32[5,32,16,128]{3,1,2,0:T(8,128)}, u32[]{:S(2)}) copy-start(f32[5,32,16,128]{3,1,2,0:T(8,128)} %get-tuple-element.112) | copy-start | bytes 3932164
  100.1 9.9 %copy-start.7 = (f32[3,32,16,128]{3,1,2,0:T(8,128)S(1)}, f32[3,32,16,128]{3,1,2,0:T(8,128)}, u32[]{:S(2)}) copy-start(f32[3,32,16,128]{3,1,2,0:T(8,128)} %get-tuple-element.113) | copy-start | bytes 2359300
  100.1 9.9 %copy-start.8 = (f32[3,32,16,128]{3,1,2,0:T(8,128)S(1)}, f32[3,32,16,128]{3,1,2,0:T(8,128)}, u32[]{:S(2)}) copy-start(f32[3,32,16,128]{3,1,2,0:T(8,128)} %get-tuple-element.114) | copy-start | bytes 2359300
  100.1 9.9 %copy-start.9 = (f32[3,32,16,128]{3,1,2,0:T(8,128)S(1)}, f32[3,32,16,128]{3,1,2,0:T(8,128)}, u32[]{:S(2)}) copy-start(f32[3,32,16,128]{3,1,2,0:T(8,128)} %get-tuple-element.62) | copy-start | bytes 2359300
  100.1 9.9 %copy-start.10 = (f32[3,32,16,128]{3,1,2,0:T(8,128)S(1)}, f32[3,32,16,128]{3,1,2,0:T(8,128)}, u32[]{:S(2)}) copy-start(f32[3,32,16,128]{3,1,2,0:T(8,128)} %get-tuple-element.107) | copy-start | bytes 2359300
  100.1 9.9 %copy-start.11 = (f32[3,32,16,128]{3,1,2,0:T(8,128)S(1)}, f32[3,32,16,128]{3,1,2,0:T(8,128)}, u32[]{:S(2)}) copy-start(f32[3,32,16,128]{3,1,2,0:T(8,128)} %get-tuple-element.108) | copy-start | bytes 2359300
  100.1 9.9 %copy-start.15 = (f32[1,32,16,128]{3,1,2,0:T(8,128)S(1)}, f32[1,32,16,128]{3,1,2,0:T(8,128)}, u32[]{:S(2)}) copy-start(f32[1,32,16,128]{3,1,2,0:T(8,128)} %get-tuple-element.68) | copy-start | bytes 786436
  100.2 9.9 %copy-start.16 = (f32[1,32,16,128]{3,1,2,0:T(8,128)S(1)}, f32[1,32,16,128]{3,1,2,0:T(8,128)}, u32[]{:S(2)}) copy-start(f32[1,32,16,128]{3,1,2,0:T(8,128)} %get-tuple-element.70) | copy-start | bytes 786436
  100.2 9.9 %copy-start.17 = (f32[1,32,16,128]{3,1,2,0:T(8,128)S(1)}, f32[1,32,16,128]{3,1,2,0:T(8,128)}, u32[]{:S(2)}) copy-start(f32[1,32,16,128]{3,1,2,0:T(8,128)} %get-tuple-element.71) | copy-start | bytes 786436
  100.2 9.9 %copy-start.18 = (f32[1,32,16,128]{3,1,2,0:T(8,128)S(1)}, f32[1,32,16,128]{3,1,2,0:T(8,128)}, u32[]{:S(2)}) copy-start(f32[1,32,16,128]{3,1,2,0:T(8,128)} %get-tuple-element.73) | copy-start | bytes 786436
  100.2 9.9 %copy-start.22 = (f32[1,32,16,128]{3,1,2,0:T(8,128)S(1)}, f32[1,32,16,128]{3,1,2,0:T(8,128)}, u32[]{:S(2)}) copy-start(f32[1,32,16,128]{3,1,2,0:T(8,128)} %negate_bitcast_fusion) | copy-start | bytes 786436
  100.2 9.9 %copy-start.23 = (f32[1,32,16,128]{3,1,2,0:T(8,128)S(1)}, f32[1,32,16,128]{3,1,2,0:T(8,128)}, u32[]{:S(2)}) copy-start(f32[1,32,16,128]{3,1,2,0:T(8,128)} %get-tuple-element.64) | copy-start | bytes 786436
  103.6 9.2 %collective-permute-start.5 = (f32[5,4,16,128]{3,1,2,0:T(4,128)S(1)}, f32[5,4,16,128]{3,1,2,0:T(4,128)S(1)}, u32[]{:S(2)}, u32[]{:S(2)}) collective-permute-start(f32[5,4,16,128]{3,1,2,0:T(4,128)S(1)} %get-tuple-element.79), channel_id=1, source_target_pairs={{0,4},{4,8},{8,12},{12,16},{16,20},{20,24},{24,28},{1,5},{5,9},{9,... | collective-permute-start | bytes 491528 | tf_op jit(solution)/shard_map/ppermute | solution.py:19
  105.5 10.5 %collective-permute-start.6 = (f32[5,4,16,128]{3,1,2,0:T(4,128)S(1)}, f32[5,4,16,128]{3,1,2,0:T(4,128)S(1)}, u32[]{:S(2)}, u32[]{:S(2)}) collective-permute-start(f32[5,4,16,128]{3,1,2,0:T(4,128)S(1)} %get-tuple-element.80), channel_id=1, source_target_pairs={{4,0},{8,4},{12,8},{16,12},{20,16},{24,20},{28,24},{5,1},{9,5},{13... | collective-permute-start | bytes 491528 | tf_op jit(solution)/shard_map/ppermute | solution.py:21
  (19 other events, 64.9 us)
where the time goes:
time: 120 us; the launch traced here: 119 us
  starting transfers between devices  38.6 us (32%)
  local copies, waits for them, and re-layouts  31.1 us (26%)
  matrix products  24.6 us (20%)
  other arithmetic  17.4 us (14%)
  waiting for transfers between devices  5.98 us (5%)
  between operations  1.36 us (1%)
    ppermute x6, starting transfers between devices, extended(): lax.ppermute(head, axis, [((i + 1) % count, i) for i in range(ends)])  25.6 us
    unnamed x82, local copies, waits for them, and re-layouts  16.5 us
    ppermute x6, starting transfers between devices, extended(): lax.ppermute(tail, axis, [(i, (i + 1) % count) for i in range(ends)])  11.4 us
    dot_general x4, matrix products, along_x(): return jnp.einsum('vard,ai->vird', ext, band, precision=highest)  11.1 us
    dot_general x2, matrix products, along_t(): return jnp.einsum('vxra,ai->vxri', ext, band, precision=highest)  8.77 us
    dot_general x2, matrix products, along_r(): return jnp.einsum('vxad,ai->vxid', ext, band, precision=highest)  4.7 us
    ppermute x6, waiting for transfers between devices, extended(): lax.ppermute(head, axis, [((i + 1) % count, i) for i in range(ends)])  4.28 us
    slice x2, local copies, waits for them, and re-layouts, shards(): flux_t[..., cells_t - reach:]  4.03 us
  transfers between devices with their start and end apart: 14, of which 3 were waited for; matrix products, arithmetic and copies ran while one was open for 33% of the time, Pallas kernels for 0%

commit v1 on v0

v1 whole, which is shorter than its diff:
```python
import functools

import jax
import jax.numpy as jnp
from jax import lax
from jax.experimental import pallas as pl
from jax.experimental.pallas import tpu as pltpu
from jax.sharding import PartitionSpec as P

section_dt = 0.1
gamma_less = 0.4
highest = lax.Precision.HIGHEST
MESH = pl.DeviceIdType.MESH
PAD = 8


def velocities(q):
    inv = 1.0 / q[0]
    vel = [q[1 + k] * inv for k in range(3)]
    kinetic = q[1] * vel[0] + q[2] * vel[1] + q[3] * vel[2]
    pressure = gamma_less * (q[4] - 0.5 * kinetic)
    return inv, vel, pressure, q[4] + pressure


def pull_back(q, grads):
    inv, vel, _, enthalpy = velocities(q)
    mom = q[1:4]
    a_enth = sum(grads[d][4] * vel[d] for d in range(3))
    a_pres = grads[0][1] + grads[1][2] + grads[2][3] + a_enth
    half = 0.5 * gamma_less * a_pres
    a_vel = [
        mom[0] * grads[d][1] + mom[1] * grads[d][2] + mom[2] * grads[d][3]
        + enthalpy * grads[d][4] - half * mom[d]
        for d in range(3)
    ]
    scaled = [a * inv for a in a_vel]
    a_mom = [
        grads[0][1 + k] * vel[0] + grads[1][1 + k] * vel[1] + grads[2][1 + k] * vel[2]
        + grads[k][0] - half * vel[k] + scaled[k]
        for k in range(3)
    ]
    a_dens = -(scaled[0] * vel[0] + scaled[1] * vel[1] + scaled[2] * vel[2])
    return [a_dens] + a_mom + [a_enth + gamma_less * a_pres]


def kernel(
    counts, state, seed, coef_x, coef_r, coef_t, coef_f, metric, new_out, adj_out,
    ST, SEED, FX, FR, FT, LAM, SEC, SSEND, TT, NEW, ADJ, BAND, MET, RIM, HALO,
    local_sem, send_sem, recv_sem,
):
    comps, X, R, T = state.shape
    taps = coef_x.shape[0]
    W = (taps - 1) // 2
    rim = 2 * W
    G = T // rim
    nx, nr = counts
    gx, row, th = lax.axis_index("gx"), lax.axis_index("row"), lax.axis_index("th")
    has_l, has_r = gx > 0, gx < nx - 1
    has_d, has_u = row > 0, row < nr - 1
    left, right = {"gx": lax.rem(gx + nx - 1, nx)}, {"gx": lax.rem(gx + 1, nx)}
    down, up = {"row": lax.rem(row + nr - 1, nr)}, {"row": lax.rem(row + 1, nr)}
    partner = {"th": 1 - th}

    load_state = pltpu.make_async_copy(state, ST, local_sem.at[0])
    load_seed = pltpu.make_async_copy(seed, SEED.at[:, pl.ds(2 * W, X)], local_sem.at[1])
    load_state.start()
    load_seed.start()

    barrier = pltpu.get_barrier_semaphore()
    for cond, device in ((has_l, left), (has_r, right), (has_d, down), (has_u, up)):
        @pl.when(cond)
        def _(device=device):
            pl.semaphore_signal(barrier, inc=1, device_id=device, device_id_type=MESH)
    pl.semaphore_signal(barrier, inc=1, device_id=partner, device_id_type=MESH)

    cx = [coef_x[j] for j in range(taps)]
    cr = [coef_r[j] for j in range(taps)]
    ct = [coef_t[j] for j in range(taps)]
    cf = [coef_f[j] for j in range(taps)]
    dx = [-section_dt * c for c in cx]
    dr = [-section_dt * c for c in cr]

    def remote(src, dst, k, device):
        return pltpu.make_async_remote_copy(
            src_ref=src, dst_ref=dst, send_sem=send_sem.at[k], recv_sem=recv_sem.at[k],
            device_id=device, device_id_type=MESH,
        )

    seed_up = remote(seed.at[:, pl.ds(X - 2 * W, 2 * W)], SEED.at[:, pl.ds(0, 2 * W)], 0, right)
    seed_dn = remote(seed.at[:, pl.ds(0, 2 * W)], SEED.at[:, pl.ds(X + 2 * W, 2 * W)], 1, left)
    fx_up = remote(FX.at[:, pl.ds(X, W)], FX.at[:, pl.ds(0, W)], 2, right)
    fx_dn = remote(FX.at[:, pl.ds(W, W)], FX.at[:, pl.ds(X + W, W)], 3, left)
    sec_up = remote(SSEND.at[1], SEC.at[:, pl.ds(0, W)], 4, right)
    sec_dn = remote(SSEND.at[0], SEC.at[:, pl.ds(X + W, W)], 5, left)
    fr_up = remote(FR.at[:, :, pl.ds(R, PAD)], FR.at[:, :, pl.ds(0, PAD)], 6, up)
    fr_dn = remote(FR.at[:, :, pl.ds(PAD, PAD)], FR.at[:, :, pl.ds(PAD + R, PAD)], 7, down)
    own_x = pl.ds(W, X)
    lam_up = remote(LAM.at[:, own_x, pl.ds(R, PAD)], LAM.at[:, own_x, pl.ds(0, PAD)], 8, up)
    lam_dn = remote(
        LAM.at[:, own_x, pl.ds(PAD, PAD)], LAM.at[:, own_x, pl.ds(PAD + R, PAD)], 9, down
    )
    ft_rim = remote(RIM.at[0], HALO.at[0], 10, partner)
    lam_rim = remote(RIM.at[1], HALO.at[1], 11, partner)

    def both(up_copy, dn_copy, lower, upper, what):
        if what == "start":
            pl.when(upper)(up_copy.start)
            pl.when(lower)(dn_copy.start)
        elif what == "recv":
            pl.when(lower)(up_copy.wait_recv)
            pl.when(upper)(dn_copy.wait_recv)
        else:
            pl.when(upper)(up_copy.wait_send)
            pl.when(lower)(dn_copy.wait_send)

    arrivals = sum(c.astype(jnp.int32) for c in (has_l, has_r, has_d, has_u)) + 1
    pl.semaphore_wait(barrier, arrivals)
    both(seed_up, seed_dn, has_l, has_r, "start")

    load_state.wait()

    def flux_step(x, _):
        q = [ST[v, x] for v in range(comps)]
        _, vel, pressure, enthalpy = velocities(q)
        for d in range(3):
            f = [q[1 + d]] + [q[1 + k] * vel[d] for k in range(3)] + [enthalpy * vel[d]]
            f[1 + d] = f[1 + d] + pressure
            for v in range(comps):
                if d == 0:
                    FX[v, x + W] = f[v]
                elif d == 1:
                    FR[v, x, pl.ds(PAD, R)] = f[v]
                else:
                    FT[v, x] = f[v]
        return 0

    lax.fori_loop(0, X, flux_step, 0)
    both(fr_up, fr_dn, has_d, has_u, "start")

    lane = lax.broadcasted_iota(jnp.int32, (R, T), 1) // rim

    def pack(slot, read):
        def step(v, _):
            for g in range(X // G):
                acc = jnp.zeros((R, T), jnp.float32)
                for k in range(G):
                    rolled = pltpu.roll(read(v, g * G + k), (rim * k + W) % T, 1)
                    acc = jnp.where(lane == k, rolled, acc)
                RIM[slot, v, g] = acc
            return 0
        lax.fori_loop(0, comps, step, 0)

    pack(0, lambda v, x: FT[v, x])
    ft_rim.start()
    both(fx_up, fx_dn, has_l, has_r, "start")

    def clear(cond, ref, index):
        @pl.when(cond)
        def _():
            def step(v, _):
                target = ref.at[v].at[index]
                target[...] = jnp.zeros(target.shape, jnp.float32)
                return 0
            lax.fori_loop(0, comps, step, 0)

    no_l, no_r, no_d, no_u = gx == 0, gx == nx - 1, row == 0, row == nr - 1
    everything = pl.ds(0, R)
    clear(no_l, SEED, (pl.ds(0, 2 * W),))
    clear(no_r, SEED, (pl.ds(X + 2 * W, 2 * W),))
    clear(no_l, FX, (pl.ds(0, W),))
    clear(no_r, FX, (pl.ds(X + W, W),))
    clear(no_l, SEC, (pl.ds(0, W),))
    clear(no_r, SEC, (pl.ds(X + W, W),))
    clear(no_d, FR, (pl.ds(0, X), pl.ds(0, PAD)))
    clear(no_u, FR, (pl.ds(0, X), pl.ds(PAD + R, PAD)))
    clear(no_d, LAM, (own_x, pl.ds(0, PAD)))
    clear(no_u, LAM, (own_x, pl.ds(PAD + R, PAD)))

    k_at = lax.broadcasted_iota(jnp.int32, (2 * T, T), 0)
    n_at = lax.broadcasted_iota(jnp.int32, (2 * T, T), 1)
    position = jnp.where(k_at < T, k_at, jnp.where(k_at < T + W, k_at - T - W, k_at - W))
    offset = jnp.where(k_at < T + rim, position - n_at, 2 * T)
    for slot in range(2):
        band = jnp.zeros((2 * T, T), jnp.float32)
        for j in range(taps):
            hit = offset == ((j - W) if slot == 0 else (W - j))
            band = jnp.where(hit, ct[j], band)
        BAND[slot] = band
    row_at = lax.broadcasted_iota(jnp.int32, (R, T), 0)
    weight = jnp.zeros((R, T), jnp.float32)
    for i in range(R):
        weight = jnp.where(row_at == i, metric[i], weight)
    MET[...] = -section_dt * weight

    def azimuthal(slot, read):
        def step(v, _):
            for g in range(X // G):
                own = read(v, g * G).reshape(G * R, T)
                halo = HALO[slot, v, g]
                rims = jnp.concatenate(
                    [halo if k == 0 else pltpu.roll(halo, T - rim * k, 1) for k in range(G)], axis=0
                )
                out = jnp.dot(
                    jnp.concatenate([own, rims], axis=1), BAND[slot],
                    precision=highest, preferred_element_type=jnp.float32,
                )
                TT[v, pl.ds(g * G, G)] = out.reshape(G, R, T) * MET[...][None]
            return 0
        lax.fori_loop(0, comps, step, 0)

    def lam_block(v, at, count):
        block = SEED[v, pl.ds(at, count + 2 * W)]
        total = block[W : W + count]
        for j in range(taps):
            total = total - cf[taps - 1 - j] * block[j : j + count]
        LAM[v, pl.ds(at, count), pl.ds(PAD, R)] = total

    load_seed.wait()

    def lam_inner(v, _):
        def step(c, _):
            lam_block(v, 2 * W + c * W, W)
            return 0
        return lax.fori_loop(0, (X - 2 * W) // W, step, 0)

    lax.fori_loop(0, comps, lam_inner, 0)

    both(fr_up, fr_dn, has_d, has_u, "recv")
    ft_rim.wait_recv()
    azimuthal(0, lambda v, x: FT[v, pl.ds(x, G)])

    def section_at(v, x, lo, hi):
        total = ST[v, x] + TT[v, x]
        for j in range(taps):
            total = total + dr[j] * FR[v, x, pl.ds(PAD - W + j, R)]
        for j in range(lo, hi):
            total = total + dx[j] * FX[v, x + j]
        return total

    def section_edge(v, _):
        for o in range(W):
            low = section_at(v, o, W - o, taps)
            SSEND[0, v, o] = low
            SEC[v, W + o] = low
            x = X - W + o
            high = section_at(v, x, 0, taps - 1 - o)
            SSEND[1, v, o] = high
            SEC[v, W + x] = high
        return 0

    lax.fori_loop(0, comps, section_edge, 0)
    both(sec_up, sec_dn, has_l, has_r, "start")

    def section_inner(v, _):
        def step(c, _):
            for o in range(2):
                x = W + 2 * c + o
                SEC[v, W + x] = section_at(v, x, 0, taps)
            return 0
        return lax.fori_loop(0, (X - 2 * W) // 2, step, 0)

    lax.fori_loop(0, comps, section_inner, 0)

    both(seed_up, seed_dn, has_l, has_r, "recv")

    def lam_edges(v, _):
        for at in (0, W, X, X + W):
            lam_block(v, at, W)
        return 0

    lax.fori_loop(0, comps, lam_edges, 0)
    clear(no_l, LAM, (pl.ds(0, W), pl.ds(PAD, R)))
    clear(no_r, LAM, (pl.ds(X + W, W), pl.ds(PAD, R)))
    both(lam_up, lam_dn, has_d, has_u, "start")
    pack(1, lambda v, x: LAM[v, x + W, pl.ds(PAD, R)])
    lam_rim.start()

    both(fx_up, fx_dn, has_l, has_r, "recv")

    def section_rest(v, _):
        for o in range(W):
            low = SEC[v, W + o]
            for j in range(W - o):
                low = low + dx[j] * FX[v, o + j]
            SEC[v, W + o] = low
            x = X - W + o
            high = SEC[v, W + x]
            for j in range(taps - 1 - o, taps):
                high = high + dx[j] * FX[v, x + j]
            SEC[v, W + x] = high
        return 0

    lax.fori_loop(0, comps, section_rest, 0)

    def new_block(v, x, count):
        block = SEC[v, pl.ds(x, count + 2 * W)]
        total = block[W : W + count]
        for j in range(taps):
            total = total - cf[j] * block[j : j + count]
        NEW[v, pl.ds(x, count)] = total

    def new_inner(v, _):
        def step(c, _):
            new_block(v, W + c * W, W)
            return 0
        return lax.fori_loop(0, (X - 2 * W) // W, step, 0)

    lax.fori_loop(0, comps, new_inner, 0)
    inner = pl.ds(W, X - 2 * W)
    store_inner = pltpu.make_async_copy(NEW.at[:, inner], new_out.at[:, inner], local_sem.at[2])
    store_inner.start()

    both(lam_up, lam_dn, has_d, has_u, "recv")
    lam_rim.wait_recv()
    azimuthal(1, lambda v, x: LAM[v, pl.ds(x + W, G), pl.ds(PAD, R)])

    def adjoint_step(x, _):
        q = [ST[v, x] for v in range(comps)]
        grads = [[], [], []]
        for v in range(comps):
            along_x = dx[taps - 1] * LAM[v, x, pl.ds(PAD, R)]
            along_r = dr[taps - 1] * LAM[v, x + W, pl.ds(PAD - W, R)]
            for j in range(1, taps):
                along_x = along_x + dx[taps - 1 - j] * LAM[v, x + j, pl.ds(PAD, R)]
                along_r = along_r + dr[taps - 1 - j] * LAM[v, x + W, pl.ds(PAD - W + j, R)]
            grads[0].append(along_x)
            grads[1].append(along_r)
            grads[2].append(TT[v, x])
        result = pull_back(q, grads)
        for v in range(comps):
            ADJ[v, x] = LAM[v, x + W, pl.ds(PAD, R)] + result[v]
        return 0

    lax.fori_loop(0, X, adjoint_step, 0)
    store_adj = pltpu.make_async_copy(ADJ, adj_out, local_sem.at[3])
    store_adj.start()

    both(sec_up, sec_dn, has_l, has_r, "recv")

    @pl.when(has_l)
    def _():
        def step(v, _):
            for o in range(W):
                total = SEC[v, o]
                for j in range(taps - 1 - o, taps):
                    total = total + dx[j] * FX[v, o + j - W]
                SEC[v, o] = total
            return 0
        lax.fori_loop(0, comps, step, 0)

    @pl.when(has_r)
    def _():
        def step(v, _):
            for o in range(W):
                total = SEC[v, X + W + o]
                for j in range(W - o):
                    total = total + dx[j] * FX[v, X + o + j]
                SEC[v, X + W + o] = total
            return 0
        lax.fori_loop(0, comps, step, 0)

    def new_edges(v, _):
        new_block(v, 0, W)
        new_block(v, X - W, W)
        return 0

    lax.fori_loop(0, comps, new_edges, 0)
    low, high = pl.ds(0, W), pl.ds(X - W, W)
    store_low = pltpu.make_async_copy(NEW.at[:, low], new_out.at[:, low], local_sem.at[4])
    store_high = pltpu.make_async_copy(NEW.at[:, high], new_out.at[:, high], local_sem.at[5])
    store_low.start()
    store_high.start()

    both(seed_up, seed_dn, has_l, has_r, "send")
    both(fx_up, fx_dn, has_l, has_r, "send")
    both(sec_up, sec_dn, has_l, has_r, "send")
    both(fr_up, fr_dn, has_d, has_u, "send")
    both(lam_up, lam_dn, has_d, has_u, "send")
    ft_rim.wait_send()
    lam_rim.wait_send()
    store_inner.wait()
    store_adj.wait()
    store_low.wait()
    store_high.wait()


def shards(state, adjoint_seed, coef_x, coef_r, coef_t, coef_filter, metric):
    comps, X, R, T = state.shape
    W = (coef_x.shape[0] - 1) // 2
    G = T // (2 * W)
    counts = (lax.axis_size("gx"), lax.axis_size("row"))
    anywhere = pl.BlockSpec(memory_space=pl.ANY)
    scalars = pl.BlockSpec(memory_space=pltpu.SMEM)
    f32 = jnp.float32
    shape = jax.ShapeDtypeStruct(state.shape, f32)
    return pl.pallas_call(
        functools.partial(kernel, counts),
        out_shape=(shape, shape),
        in_specs=[anywhere, anywhere] + [scalars] * 5,
        out_specs=(anywhere, anywhere),
        scratch_shapes=[
            pltpu.VMEM((comps, X, R, T), f32),
            pltpu.VMEM((comps, X + 4 * W, R, T), f32),
            pltpu.VMEM((comps, X + 2 * W, R, T), f32),
            pltpu.VMEM((comps, X, R + 2 * PAD, T), f32),
            pltpu.VMEM((comps, X, R, T), f32),
            pltpu.VMEM((comps, X + 2 * W, R + 2 * PAD, T), f32),
            pltpu.VMEM((comps, X + 2 * W, R, T), f32),
            pltpu.VMEM((2, comps, W, R, T), f32),
            pltpu.VMEM((comps, X, R, T), f32),
            pltpu.VMEM((comps, X, R, T), f32),
            pltpu.VMEM((comps, X, R, T), f32),
            pltpu.VMEM((2, 2 * T, T), f32),
            pltpu.VMEM((R, T), f32),
            pltpu.VMEM((2, comps, X // G, R, T), f32),
            pltpu.VMEM((2, comps, X // G, R, T), f32),
            pltpu.SemaphoreType.DMA((6,)),
            pltpu.SemaphoreType.DMA((12,)),
            pltpu.SemaphoreType.DMA((12,)),
        ],
        compiler_params=pltpu.CompilerParams(
            collective_id=0, has_side_effects=True, vmem_limit_bytes=40 * 2**20
        ),
    )(state, adjoint_seed, coef_x, coef_r, coef_t, coef_filter, metric)


def solution(mesh):
    placed = (P(None, "gx", "row", "th"), P(None, "gx", "row", "th"), P(), P(), P(), P(), P("row"))
    return jax.shard_map(
        shards,
        mesh=mesh,
        in_specs=placed,
        out_specs=(P(None, "gx", "row", "th"), P(None, "gx", "row", "th")),
        check_vma=False,
    )
```

time: 120 us -> 46.6 us (0.39)
  starting transfers between devices: 38.6 us -> 0 us
  Pallas kernels: 0 us -> 37.2 us
  matrix products: 24.6 us -> 0 us
  local copies, waits for them, and re-layouts: 31.1 us -> 8.01 us
  other arithmetic: 17.4 us -> 0 us
  waiting for transfers between devices: 5.98 us -> 0 us
    ppermute x14 -> x0, starting transfers between devices: 38.6 us -> none  [the longest x6 25.6 us: extended(): lax.ppermute(head, axis, [((i + 1) % count, i) for i in range(ends)])]
    pallas_call x0 -> x1, Pallas kernels: none -> 37.2 us  [shards(): pl.pallas_call(functools.partial(kernel, counts), out_shape=(shape, shape...]
    dot_general x8 -> x0, matrix products: 24.6 us -> none  [the longest x4 11.1 us: along_x(): return jnp.einsum('vard,ai->vird', ext, band, precision=highest)]
    slice x12 -> x0, local copies, waits for them, and re-layouts: 13.4 us -> none  [the longest x2 4.03 us: shards(): flux_t[..., cells_t - reach:]]
    unnamed x82 -> x16, local copies, waits for them, and re-layouts: 16.5 us -> 8.01 us
    ppermute x14 -> x0, waiting for transfers between devices: 5.98 us -> none  [the longest x6 4.28 us: extended(): lax.ppermute(head, axis, [((i + 1) % count, i) for i in range(ends)])]
    concatenate x5 -> x0, other arithmetic: 3.76 us -> none  [the longest x2 2.47 us: extended(): jnp.concatenate([lax.ppermute(tail, axis, [(i, (i + 1) % count) for i in...]
    reduce_sum x4 -> x0, other arithmetic: 2.77 us -> none  [the longest x3 2.28 us: band_matrix(): return jnp.sum(jnp.where(hits, coef[:, None, None], 0.0), axis=0)]
  transfers between devices with their start and end apart: 14 -> 0, of which waited for: 3 -> 0; matrix products, arithmetic and copies ran while one was open for 33% -> 0% of each run, Pallas kernels for 0% -> 0%
where the time goes in v1:
time: 46.6 us; the launch traced here: 45.9 us
  Pallas kernels  37.2 us (80%)
  local copies, waits for them, and re-layouts  8.01 us (17%)
  between operations  0.66 us (1%)
    pallas_call x1, Pallas kernels, shards(): pl.pallas_call(functools.partial(kernel, counts), out_shape=(shape, shape...  37.2 us
    unnamed x16, local copies, waits for them, and re-layouts  8.01 us

profile of v1, /device:TPU:9, one launch (start us, length us, event | category | flops | bytes accessed | tf_op | source)
XLA Modules:
  0.0 45.9 jit_solution(13560700595060372232)
XLA Ops:
  0.6 0.0 copy-start
  0.6 1.3 %copy-done = f32[5,32,16,128]{3,2,1,0:T(8,128)S(1)} copy-done((f32[5,32,16,128]{3,2,1,0:T(8,128)S(1)}, f32[5,32,16,128]{3,2,1,0:T(8,128)}, u32[]{:S(2)}) %copy-start) | copy-done | bytes 1310744
  1.9 0.0 copy-start.1
  2.0 1.3 %copy-done.1 = f32[5,32,16,128]{3,2,1,0:T(8,128)S(1)} copy-done((f32[5,32,16,128]{3,2,1,0:T(8,128)S(1)}, f32[5,32,16,128]{3,2,1,0:T(8,128)}, u32[]{:S(2)}) %copy-start.1) | copy-done | bytes 1310744
  3.3 0.0 copy-start.2
  3.3 0.7 %copy-done.2 = f32[9]{0:T(128)S(1)} copy-done((f32[9]{0:T(128)S(1)}, f32[9]{0:T(128)}, u32[]{:S(2)}) %copy-start.2) | copy-done | bytes 60
  3.9 0.0 copy-start.3
  3.9 0.7 %copy-done.3 = f32[9]{0:T(128)S(1)} copy-done((f32[9]{0:T(128)S(1)}, f32[9]{0:T(128)}, u32[]{:S(2)}) %copy-start.3) | copy-done | bytes 60
  4.6 0.0 copy-start.4
  4.6 0.7 %copy-done.4 = f32[9]{0:T(128)S(1)} copy-done((f32[9]{0:T(128)S(1)}, f32[9]{0:T(128)}, u32[]{:S(2)}) %copy-start.4) | copy-done | bytes 60
  5.2 0.0 copy-start.5
  5.2 0.7 %copy-done.5 = f32[9]{0:T(128)S(1)} copy-done((f32[9]{0:T(128)S(1)}, f32[9]{0:T(128)}, u32[]{:S(2)}) %copy-start.5) | copy-done | bytes 60
  5.9 0.0 copy-start.6
  5.9 0.7 %copy-done.6 = f32[16]{0:T(128)S(1)} copy-done((f32[16]{0:T(128)S(1)}, f32[16]{0:T(128)}, u32[]{:S(2)}) %copy-start.6) | copy-done | bytes 88
  6.5 37.2 %shard_map.86 = (f32[5,32,16,128]{3,2,1,0:T(8,128)S(1)}, f32[5,32,16,128]{3,2,1,0:T(8,128)S(1)}) custom-call(f32[5,32,16,128]{3,2,1,0:T(8,128)S(1)} %copy-done, f32[5,32,16,128]{3,2,1,0:T(8,128)S(1)} %copy-done.1, f32[9]{0:T(128)S(1)} %copy-done.2, f32[9]{0:T(128)S(1)} %copy-done.3, f32[9]{0:T(128)S(1)} %copy-done.4, f32[9]{0:T(128)S(1)} %copy-done.5, ...), custom_call_target="tpu_custom_call" | custom-call | tf_op jit(solution)/shard_map/pallas_call | solution.py:396
  43.8 1.1 %copy.11 = f32[5,32,16,128]{3,2,1,0:T(8,128)} copy(f32[5,32,16,128]{3,2,1,0:T(8,128)S(1)} %get-tuple-element.4) | data formatting | bytes 2621440
  44.8 1.1 %copy.12 = f32[5,32,16,128]{3,2,1,0:T(8,128)} copy(f32[5,32,16,128]{3,2,1,0:T(8,128)S(1)} %get-tuple-element.5) | data formatting | bytes 2621440
Async XLA Ops:
  0.6 1.3 %copy-start = (f32[5,32,16,128]{3,2,1,0:T(8,128)S(1)}, f32[5,32,16,128]{3,2,1,0:T(8,128)}, u32[]{:S(2)}) copy-start(f32[5,32,16,128]{3,2,1,0:T(8,128)} %state.1) | copy-start | bytes 3932164
  1.9 1.3 %copy-start.1 = (f32[5,32,16,128]{3,2,1,0:T(8,128)S(1)}, f32[5,32,16,128]{3,2,1,0:T(8,128)}, u32[]{:S(2)}) copy-start(f32[5,32,16,128]{3,2,1,0:T(8,128)} %seed.1) | copy-start | bytes 3932164
  3.3 0.7 %copy-start.2 = (f32[9]{0:T(128)S(1)}, f32[9]{0:T(128)}, u32[]{:S(2)}) copy-start(f32[9]{0:T(128)} %coef_x.1) | copy-start | bytes 112
  3.9 0.7 %copy-start.3 = (f32[9]{0:T(128)S(1)}, f32[9]{0:T(128)}, u32[]{:S(2)}) copy-start(f32[9]{0:T(128)} %coef_r.1) | copy-start | bytes 112
  4.6 0.7 %copy-start.4 = (f32[9]{0:T(128)S(1)}, f32[9]{0:T(128)}, u32[]{:S(2)}) copy-start(f32[9]{0:T(128)} %coef_t.1) | copy-start | bytes 112
  5.2 0.7 %copy-start.5 = (f32[9]{0:T(128)S(1)}, f32[9]{0:T(128)}, u32[]{:S(2)}) copy-start(f32[9]{0:T(128)} %coef_f.1) | copy-start | bytes 112
  5.9 0.7 %copy-start.6 = (f32[16]{0:T(128)S(1)}, f32[16]{0:T(128)}, u32[]{:S(2)}) copy-start(f32[16]{0:T(128)} %metric.1) | copy-start | bytes 196

commit v2 on v1

--- a/solution.py
+++ b/solution.py
@@ -9,7 +9,6 @@
 
 section_dt = 0.1
 gamma_less = 0.4
-highest = lax.Precision.HIGHEST
 MESH = pl.DeviceIdType.MESH
 PAD = 8
 
@@ -135,6 +134,7 @@
         return 0
 
     lax.fori_loop(0, X, flux_step, 0)
+    both(fx_up, fx_dn, has_l, has_r, "start")
     both(fr_up, fr_dn, has_d, has_u, "start")
 
     lane = lax.broadcasted_iota(jnp.int32, (R, T), 1) // rim
@@ -152,7 +152,6 @@
 
     pack(0, lambda v, x: FT[v, x])
     ft_rim.start()
-    both(fx_up, fx_dn, has_l, has_r, "start")
 
     def clear(cond, ref, index):
         @pl.when(cond)
@@ -185,7 +184,9 @@
         for j in range(taps):
             hit = offset == ((j - W) if slot == 0 else (W - j))
             band = jnp.where(hit, ct[j], band)
-        BAND[slot] = band
+        upper = band.astype(jnp.bfloat16)
+        BAND[slot, 0] = upper
+        BAND[slot, 1] = (band - upper.astype(jnp.float32)).astype(jnp.bfloat16)
     row_at = lax.broadcasted_iota(jnp.int32, (R, T), 0)
     weight = jnp.zeros((R, T), jnp.float32)
     for i in range(R):
@@ -200,9 +201,12 @@
                 rims = jnp.concatenate(
                     [halo if k == 0 else pltpu.roll(halo, T - rim * k, 1) for k in range(G)], axis=0
                 )
-                out = jnp.dot(
-                    jnp.concatenate([own, rims], axis=1), BAND[slot],
-                    precision=highest, preferred_element_type=jnp.float32,
+                both_parts = jnp.concatenate([own, rims], axis=1)
+                upper = both_parts.astype(jnp.bfloat16)
+                lower = (both_parts - upper.astype(jnp.float32)).astype(jnp.bfloat16)
+                multiply = functools.partial(jnp.dot, preferred_element_type=jnp.float32)
+                out = multiply(upper, BAND[slot, 0]) + (
+                    multiply(lower, BAND[slot, 0]) + multiply(upper, BAND[slot, 1])
                 )
                 TT[v, pl.ds(g * G, G)] = out.reshape(G, R, T) * MET[...][None]
             return 0
@@ -249,7 +253,6 @@
         return 0
 
     lax.fori_loop(0, comps, section_edge, 0)
-    both(sec_up, sec_dn, has_l, has_r, "start")
 
     def section_inner(v, _):
         def step(c, _):
@@ -260,6 +263,9 @@
         return lax.fori_loop(0, (X - 2 * W) // 2, step, 0)
 
     lax.fori_loop(0, comps, section_inner, 0)
+
+    both(seed_up, seed_dn, has_l, has_r, "send")
+    both(sec_up, sec_dn, has_l, has_r, "start")
 
     both(seed_up, seed_dn, has_l, has_r, "recv")
 
@@ -371,7 +377,6 @@
     store_low.start()
     store_high.start()
 
-    both(seed_up, seed_dn, has_l, has_r, "send")
     both(fx_up, fx_dn, has_l, has_r, "send")
     both(sec_up, sec_dn, has_l, has_r, "send")
     both(fr_up, fr_dn, has_d, has_u, "send")
@@ -410,7 +415,7 @@
             pltpu.VMEM((comps, X, R, T), f32),
             pltpu.VMEM((comps, X, R, T), f32),
             pltpu.VMEM((comps, X, R, T), f32),
-            pltpu.VMEM((2, 2 * T, T), f32),
+            pltpu.VMEM((2, 2, 2 * T, T), jnp.bfloat16),
             pltpu.VMEM((R, T), f32),
             pltpu.VMEM((2, comps, X // G, R, T), f32),
             pltpu.VMEM((2, comps, X // G, R, T), f32),
@@ -419,7 +424,7 @@
             pltpu.SemaphoreType.DMA((12,)),
         ],
         compiler_params=pltpu.CompilerParams(
-            collective_id=0, has_side_effects=True, vmem_limit_bytes=40 * 2**20
+            collective_id=0, has_side_effects=True, vmem_limit_bytes=60 * 2**20
         ),
     )(state, adjoint_seed, coef_x, coef_r, coef_t, coef_filter, metric)
 

time: 46.6 us -> 42 us (0.901)
  local copies, waits for them, and re-layouts: 8.01 us -> 3.67 us
    unnamed x16 -> x4, local copies, waits for them, and re-layouts: 8.01 us -> 3.67 us
where the time goes in v2:
time: 42 us; the launch traced here: 41.3 us
  Pallas kernels  37 us (88%)
  local copies, waits for them, and re-layouts  3.67 us (9%)
  between operations  0.65 us (2%)
    pallas_call x1, Pallas kernels, shards(): pl.pallas_call(functools.partial(kernel, counts), out_shape=(shape, shape...  37 us
    unnamed x4, local copies, waits for them, and re-layouts  3.67 us

profile of v2, /device:TPU:9, one launch (start us, length us, event | category | flops | bytes accessed | tf_op | source)
XLA Modules:
  0.0 41.3 jit_solution(9482919376554765511)
XLA Ops:
  0.6 37.0 %shard_map.86 = (f32[5,32,16,128]{3,2,1,0:T(8,128)}, f32[5,32,16,128]{3,2,1,0:T(8,128)}) custom-call(f32[5,32,16,128]{3,2,1,0:T(8,128)} %state.1, f32[5,32,16,128]{3,2,1,0:T(8,128)} %seed.1, f32[9]{0:T(128)} %coef_x.1, f32[9]{0:T(128)} %coef_r.1, f32[9]{0:T(128)} %coef_t.1, f32[9]{0:T(128)} %coef_f.1, f32[16]{0:T(128)} %metric.1), custom_call_target="tpu_custom_call" | custom-call | tf_op jit(solution)/shard_map/pallas_call | solution.py:401
  37.6 0.0 copy-start
  37.7 2.6 %copy.11 = f32[5,32,16,128]{3,2,1,0:T(8,128)} copy(f32[5,32,16,128]{3,2,1,0:T(8,128)} %get-tuple-element.4) | data formatting | bytes 2621440
  40.3 0.0 copy-done
  40.3 1.1 %copy.12 = f32[5,32,16,128]{3,2,1,0:T(8,128)} copy(f32[5,32,16,128]{3,2,1,0:T(8,128)S(1)} %copy-done) | data formatting | bytes 2621440
Async XLA Ops:
  37.6 2.6 %copy-start = (f32[5,32,16,128]{3,2,1,0:T(8,128)S(1)}, f32[5,32,16,128]{3,2,1,0:T(8,128)}, u32[]{:S(2)}) copy-start(f32[5,32,16,128]{3,2,1,0:T(8,128)} %get-tuple-element.5) | copy-start | bytes 3932164
